TPU v7x, 128 devices: a whole 4x4x4 slice. The times are simulated.
128 devices in a mesh: run: 16 (over x_hi, z, core), mz: 8 (over x_lo, y).
Axes of the slice: x: 4 (x_hi: 2, x_lo: 2; x = x_hi * 2 + x_lo), y: 4, z: 4, core: 2. Of those that a mesh axis runs over, the one named last changes fastest.
Arguments:
- lcms: bfloat16 [1024, 256, 4096], P('run', None, 'mz'), may hold values from -600 to 600
- spectra: float32 [1024, 65536], P('run', 'mz'), may hold values from -200 to 200
- scan_factor: float32 [64, 256], replicated, may hold values from 0.05 to 0.9
- mz_factor: float32 [64, 4096], P(None, 'mz'), may hold values from 0 to 1.7
- ppm_factor: float32 [64, 65536], P(None, 'mz'), may hold values from 0 to 1.7
Outputs:
- sample_factor: float32 [1024, 64], P('run')
- ppm_new: float32 [64, 65536], P(None, ('mz', 'run'))
All inputs are finite; a program needn't handle non-finite values.
Results may differ from a plain program's by a relative error of at most 0.0048.
Values sent between devices are 32-bit elements; how exact they have to be, the bound alone decides.
A program may use at most 64 MiB of HBM per device.

v0:
```python
import jax
import jax.numpy as jnp
from jax import lax
from jax.sharding import PartitionSpec as P


def solve_rows(gram_matrix, right_rows):
    lower_factor = jnp.linalg.cholesky(gram_matrix)
    return jax.scipy.linalg.cho_solve((lower_factor, True), right_rows.T).T


def per_device(lcms, spectra, scan_factor, mz_factor, ppm_factor):
    highest = lax.Precision.HIGHEST
    runs_dev = lcms.shape[0]
    rank_size = scan_factor.shape[0]
    scan_bf = scan_factor.astype(jnp.bfloat16)
    tensor = jnp.einsum("ijk,rj->irk", lcms, scan_bf, preferred_element_type=jnp.float32)
    lcms_local = jnp.sum(tensor * mz_factor[None], axis=2)
    nmr_local = lax.dot_general(spectra, ppm_factor, (((1,), (1,)), ((), ())), precision=highest)
    mz_local = jnp.dot(mz_factor, mz_factor.T, precision=highest)
    ppm_local = jnp.dot(ppm_factor, ppm_factor.T, precision=highest)
    mz_gram, ppm_gram = lax.psum((mz_local, ppm_local), "mz")
    lcms_part, nmr_part = lax.psum((lcms_local, nmr_local), "mz")
    lcms_gram = jnp.dot(scan_factor, scan_factor.T, precision=highest) * mz_gram
    sample_first = solve_rows(lcms_gram + ppm_gram, lcms_part + nmr_part)
    sample_gram = lax.psum(jnp.dot(sample_first.T, sample_first, precision=highest), "run")
    products = jnp.dot(sample_first.T, spectra, precision=highest)
    projected = lax.psum_scatter(products, "run", scatter_dimension=1, tiled=True)
    ppm_new = jax.scipy.linalg.cho_solve((jnp.linalg.cholesky(sample_gram), True), projected)
    empty_fit = jnp.zeros((runs_dev, rank_size), jnp.float32)
    empty_gram = jnp.zeros((rank_size, rank_size), jnp.float32)
    ppm_piece = lax.all_gather(ppm_new, "run", axis=1, tiled=True)
    fit_more = lax.dot_general(spectra, ppm_piece, (((1,), (1,)), ((), ())), precision=highest)
    gram_more = jnp.dot(ppm_piece, ppm_piece.T, precision=highest)
    fit_part = empty_fit + fit_more
    gram_part = empty_gram + gram_more
    nmr_fit, new_gram = lax.psum((fit_part, gram_part), "mz")
    sample_factor = solve_rows(lcms_gram + new_gram, lcms_part + nmr_fit)
    return (sample_factor, ppm_new)


def solution(mesh):
    return jax.shard_map(
        per_device,
        mesh=mesh,
        in_specs=(P("run", None, "mz"), P("run", "mz"), P(), P(None, "mz"), P(None, "mz")),
        out_specs=(P("run", None), P(None, ("mz", "run"))),
        check_vma=False,
    )
```

profile of v0, /device:TPU:0, one launch (start us, length us, event | category | flops | bytes accessed | tf_op | source)
XLA Modules:
  0.0 303.4 jit_solution(14854345805420689423)
XLA Ops:
  7.2 2.0 fusion.28
  9.2 4.8 %fusion.29 = f32[64,64]{0,1:T(8,128)} fusion(f32[64,8192]{1,0:T(8,128)} %param.12), kind=kOutput, calls=%fused_computation.45 | convolution fusion | flops 402653184 | bytes 2113536 | tf_op jit(solution)/shard_map/dot_general | solution.py:21
  14.0 2.4 fusion.30
  16.5 9.6 %multiply_reduce_fusion = f32[64,64]{0,1:T(8,128)} fusion(f32[64,512]{1,0:T(8,128)S(1)} %copy-done.3, bf16[64,256,512]{2,1,0:T(8,128)(2,1)} %param.8, f32[64,256]{1,0:T(8,128)S(1)} %copy-done.4), kind=kOutput, calls=%fused_computation | convolution fusion | flops 1077948416 | bytes 16990208 | tf_op jit(solution)/shard_map/ijk,rj->irk/dot_general | solution.py:17
  26.1 76.0 %all-reduce.4.cloned.1.call-done = (f32[64,64]{0,1:T(8,128)}, f32[64,64]{0,1:T(8,128)}, f32[64,64]{1,0:T(8,128)}, f32[64,64]{1,0:T(8,128)}) async-done(((f32[64,64]{0,1:T(8,128)}, f32[64,64]{0,1:T(8,128)}, f32[64,64]{1,0:T(8,128)}, f32[64,64]{1,0:T(8,128)}), (f32[64,64]{0,1:T(8,128)}, f32[64,64]{0,1:T(8,128)}, f32[64,64]{1,0:T(8,128)}, f32[64,64]{1,0:T(8,128)})) %all-reduce.4.cloned.1.call-update) | async-done | bytes 65552 | tf_op jit(solution)/shard_map/psum | solution.py:22
  102.2 1.0 fusion.27
  103.3 5.8 %cholesky.59 = f32[64,64]{1,0:T(8,128)S(1)} custom-call(f32[64,64]{1,0:T(8,128)S(1)} %fusion.19), custom_call_target="Cholesky" | custom-call | tf_op jit(solution)/shard_map/jit(cholesky)/cholesky | solution.py:8
  109.8 0.7 fusion
  110.5 4.9 %custom-call.16 = f32[1,64,64]{1,2,0:T(8,128)S(1)} custom-call(f32[1,64,64]{2,1,0:T(8,128)S(1)} %fusion), custom_call_target="InvertDiagBlocksLowerTriangular" | custom-call | tf_op jit(solution)/shard_map/jit(_cho_solve)/triangular_solve | solution.py:9
  115.4 1.0 fusion.13
  116.5 3.3 %fusion.32 = f32[64,8192]{1,0:T(8,128)} fusion(f32[64,64]{1,0:T(8,128)S(1)} %fusion.16, f32[64,8192]{1,0:T(8,128)S(1)} %copy-done), kind=kOutput, calls=%fused_computation.48 | convolution fusion | flops 402653184 | bytes 4210688 | tf_op jit(solution)/shard_map/dot_general | solution.py:27
  120.1 65.3 %psum.53 = f32[64,64]{0,1:T(8,128)S(1)} all-reduce(f32[64,64]{0,1:T(8,128)S(1)} %fusion.31), channel_id=1, replica_groups=mesh['run'=16,'mz'=8] {'run'}, use_global_device_ids=true, to_apply=%region_7.10 | all-reduce | flops 4096 | bytes 32768 | tf_op jit(solution)/shard_map/psum | solution.py:26
  185.5 5.8 %cholesky.70 = f32[64,64]{1,0:T(8,128)S(1)} custom-call(f32[64,64]{1,0:T(8,128)S(1)} %fusion.12), custom_call_target="Cholesky" | custom-call | tf_op jit(solution)/shard_map/jit(cholesky)/cholesky | solution.py:29
  192.0 0.7 fusion.1
  192.7 4.9 %custom-call.14 = f32[1,64,64]{1,2,0:T(8,128)S(1)} custom-call(f32[1,64,64]{2,1,0:T(8,128)S(1)} %fusion.1), custom_call_target="InvertDiagBlocksLowerTriangular" | custom-call | tf_op jit(solution)/shard_map/jit(_cho_solve)/triangular_solve | solution.py:29
  197.6 1.2 fusion.10
  198.9 0.9 fusion.8
  199.8 44.6 %all-gather.2.cloned.1.call-done = f32[64,8192]{1,0:T(8,128)} async-done(((f32[64,512]{1,0:T(8,128)}), f32[64,8192]{1,0:T(8,128)}) %all-gather.2.cloned.1.call-update) | async-done | bytes 2097168 | tf_op jit(solution)/shard_map/all_gather | solution.py:32
  244.5 3.6 %convolution_bitcast_fusion.1 = f32[64,64]{1,0:T(8,128)S(1)} fusion(f32[64,8192]{1,0:T(8,128)} %all-gather.2.cloned.1.call-done, f32[64,8192]{1,0:T(8,128)S(1)} %copy-done), kind=kOutput, calls=%fused_computation.2 | convolution fusion | flops 402653184 | bytes 4210688 | tf_op jit(solution)/shard_map/dot_general | solution.py:33
  248.0 1.8 fusion.33
  249.8 33.7 %all-reduce = (f32[64,64]{0,1:T(8,128)S(1)}, f32[64,64]{1,0:T(8,128)S(1)}) all-reduce(f32[64,64]{0,1:T(8,128)S(1)} %fusion.33, f32[64,64]{1,0:T(8,128)S(1)} %convolution_bitcast_fusion.1), channel_id=1, replica_groups=mesh['run'=16,'mz'=8] {'mz'}, use_global_device_ids=true, to_apply=%region_9.12 | all-reduce | flops 8192 | bytes 65536 | tf_op jit(solution)/shard_map/psum | solution.py:37
  283.7 5.8 %cholesky.81 = f32[64,64]{1,0:T(8,128)S(1)} custom-call(f32[64,64]{1,0:T(8,128)S(1)} %fusion.7), custom_call_target="Cholesky" | custom-call | tf_op jit(solution)/shard_map/jit(cholesky)/cholesky | solution.py:8
  290.8 4.9 %custom-call.17 = f32[1,64,64]{1,2,0:T(8,128)S(1)} custom-call(f32[1,64,64]{2,1,0:T(8,128)S(1)} %fusion.2), custom_call_target="InvertDiagBlocksLowerTriangular" | custom-call | tf_op jit(solution)/shard_map/jit(_cho_solve)/triangular_solve | solution.py:9
  296.2 0.7 copy.24
  (37 shorter events, 3.9 us)
Async XLA Ops:
  7.2 6.8 %copy-start = (f32[64,8192]{1,0:T(8,128)S(1)}, f32[64,8192]{1,0:T(8,128)}, u32[]{:S(2)}) copy-start(f32[64,8192]{1,0:T(8,128)} %param.9) | copy-start | bytes 6291460
  7.2 95.0 %all-reduce.4.cloned.1.call-start = ((), (), s32[]{:S(2)}) async-start(), calls=%async_computation.3 | async-start | bytes 262144 | tf_op jit(solution)/shard_map/psum | solution.py:22
  9.2 4.8 %copy-start.1 = (f32[64,8192]{1,0:T(8,128)S(1)}, f32[64,8192]{1,0:T(8,128)}, u32[]{:S(2)}) copy-start(f32[64,8192]{1,0:T(8,128)} %param.12) | copy-start | bytes 6291460
  14.0 2.4 copy-start.3
  14.0 2.4 copy-start.4
  26.1 171.5 %reduce-scatter.2.cloned.1.call-start = ((), (), s32[]{:S(2)}) async-start(), calls=%async_computation.1 | async-start | bytes 2228224 | tf_op jit(solution)/shard_map/reduce_scatter | solution.py:28
  119.8 124.6 %all-gather.2.cloned.1.call-start = ((), (), s32[]{:S(2)}) async-start(), calls=%async_computation.2 | async-start | bytes 2228224 | tf_op jit(solution)/shard_map/all_gather | solution.py:32
  244.5 3.6 %copy-start.2 = (f32[64,8192]{1,0:T(8,128)S(1)}, f32[64,8192]{1,0:T(8,128)}, u32[]{:S(2)}) copy-start(f32[64,8192]{1,0:T(8,128)} %all-gather.2.cloned.1.call-done) | copy-start | bytes 6291460
  248.0 47.7 %copy-start.5 = (f32[64,64]{1,0:T(8,128)S(1)}, f32[64,64]{1,0:T(8,128)}, u32[]{:S(2)}) copy-start(f32[64,64]{1,0:T(8,128)} %get-tuple-element.12) | copy-start | bytes 49156
Sparse Core Ops, SparseCore 0:
  26.2 75.9 all-reduce.3
  120.0 70.7 reduce-scatter.1
  199.9 44.4 all-gather.1
where the time goes:
time: 304 us; the launch traced here: 303 us
  waiting for transfers between devices  121 us (40%)
  blocking collectives  99 us (33%)
  other arithmetic  36.3 us (12%)
  matrix products  32.3 us (11%)
  between operations  13.9 us (5%)
    psum x1, waiting for transfers between devices, per_device(): mz_gram, ppm_gram = lax.psum((mz_local, ppm_local), 'mz')  76 us
    psum x1, blocking collectives, per_device(): lax.psum(jnp.dot(sample_first.T, sample_first, precision=highest), 'run')  65.3 us
    all_gather x1, waiting for transfers between devices, per_device(): ppm_piece = lax.all_gather(ppm_new, 'run', axis=1, tiled=True)  44.6 us
    psum x1, blocking collectives, per_device(): nmr_fit, new_gram = lax.psum((fit_part, gram_part), 'mz')  33.7 us
    another operation x6, other arithmetic, solve_rows(): lower_factor = jnp.linalg.cholesky(gram_matrix)  13 us
    another operation x4, other arithmetic, solve_rows(): return jax.scipy.linalg.cho_solve((lower_factor, True), right_rows.T).T  11.1 us
    dot_general x1, matrix products, per_device(): jnp.einsum('ijk,rj->irk', lcms, scan_bf, preferred_element_type=jnp.float32)  9.6 us
    another operation x3, other arithmetic, per_device(): jnp.linalg.cholesky(sample_gram)  6.52 us
  transfers between devices with their start and end apart: 3, of which 2 were waited for; matrix products, arithmetic and copies ran while one was open for 4% of the time, Pallas kernels for 0%

commit v1 on v0

v1 whole, which is shorter than its diff:
```python
import functools

import jax
import jax.numpy as jnp
from jax import lax
from jax.experimental import pallas as pl
from jax.experimental.pallas import tpu as pltpu
from jax.sharding import PartitionSpec as P

MESH = pl.DeviceIdType.MESH
HIGHEST = lax.Precision.HIGHEST
F32 = jnp.float32
BF16 = jnp.bfloat16
NT = (((1,), (1,)), ((), ()))
TN = (((0,), (0,)), ((), ()))
NN = (((1,), (0,)), ((), ()))

N_RUN = 16
N_MZ = 8
RANK = 64
RUNS = 64
SCANS = 256
CHANNELS = 512
POSITIONS = 8192
OWNED = 512
LCMS_PARTS = 16
FIRST_BATCH = (2, 14, 8, 1, 4, 10, 6)
SECOND_BATCH = (12, 3)
THIRD_BATCH = (15, 9, 5, 11, 7, 13)


def split(value):
    high = value.astype(BF16)
    low = (value - high.astype(F32)).astype(BF16)
    return high, low


def dot(left, right, dims, precision=None):
    return lax.dot_general(left, right, dims, precision=precision, preferred_element_type=F32)


def small_inverse(block):
    if len(block) == 2:
        scale = 1.0 / (block[0][0] * block[1][1] - block[0][1] * block[0][1])
        off = -block[0][1] * scale
        return [[block[1][1] * scale, off], [off, block[0][0] * scale]]
    half = range(2)
    upper = small_inverse([[block[i][j] for j in half] for i in half])
    cross = [[block[i][2 + j] for j in half] for i in half]
    mixed = [[upper[i][0] * cross[0][j] + upper[i][1] * cross[1][j] for j in half] for i in half]
    rest = [[None, None], [None, None]]
    for i in half:
        for j in range(i, 2):
            rest[i][j] = block[2 + i][2 + j] - (cross[0][i] * mixed[0][j] + cross[1][i] * mixed[1][j])
    rest[1][0] = rest[0][1]
    lower = small_inverse(rest)
    side = [[mixed[i][0] * lower[0][j] + mixed[i][1] * lower[1][j] for j in half] for i in half]
    result = [[None] * 4 for _ in range(4)]
    for i in half:
        for j in half:
            result[i][j] = upper[i][j] + (side[i][0] * mixed[j][0] + side[i][1] * mixed[j][1])
            result[i][2 + j] = -side[i][j]
            result[2 + j][i] = -side[i][j]
            result[2 + i][2 + j] = lower[i][j]
    return result


def spd_inverse(matrix):
    size, wide, pivot = RANK, 2 * RANK, 4
    tiles = []
    lane = lax.broadcasted_iota(jnp.int32, (8, wide), 1)
    sub = lax.broadcasted_iota(jnp.int32, (8, wide), 0)
    for t in range(size // 8):
        unit = (lane == sub + (size + 8 * t)).astype(F32)
        left = jnp.concatenate([matrix[8 * t : 8 * t + 8], jnp.zeros((8, size), F32)], axis=1)
        tiles.append(left + unit)
    for j in range(0, size, pivot):
        home, first = j // 8, j % 8
        rows = [jnp.broadcast_to(tiles[home][first + k : first + k + 1], (8, wide)) for k in range(pivot)]
        block = [[None] * pivot for _ in range(pivot)]
        for k in range(pivot):
            for m in range(k, pivot):
                block[k][m] = jnp.broadcast_to(rows[k][:, j + m : j + m + 1], (8, wide))
                block[m][k] = block[k][m]
        inverse = small_inverse(block)
        fresh = []
        for k in range(pivot):
            fresh.append((inverse[k][0] * rows[0] + inverse[k][1] * rows[1]) + (inverse[k][2] * rows[2] + inverse[k][3] * rows[3]))
        for t in range(size // 8):
            tile = tiles[t]
            taken = [jnp.broadcast_to(tile[:, j + k : j + k + 1], (8, wide)) * fresh[k] for k in range(pivot)]
            tile = tile - ((taken[0] + taken[1]) + (taken[2] + taken[3]))
            if t == home:
                for k in range(pivot):
                    tile = jnp.where(sub == first + k, fresh[k], tile)
            tiles[t] = tile
    return jnp.concatenate([tile[:, size:] for tile in tiles], axis=0)


def pack(value):
    return jnp.concatenate([value[0:32], value[32:64]], axis=1)


def unpack(value):
    return jnp.concatenate([value[:, 0:64], value[:, 64:128]], axis=0)


def twice(value):
    empty = jnp.zeros_like(value)
    return jnp.concatenate(
        [jnp.concatenate([value, empty], axis=1), jnp.concatenate([empty, value], axis=1)], axis=0
    )


def fold(value):
    wide = value[0:64] + value[64:128]
    return wide[:, 0:64] + wide[:, 64:128]


def kernel(
    lcms_hbm, spectra_hbm, scan_hbm, mz_hbm, ppm_hbm,
    sample_ref, new_ref,
    lcms_v, spectra_v, scan_v, mz_v, ppm_v, lcms_acc, columns_v,
    gram_in, right_in, right_all, fit_out, fit_in, new_gram_in, last_in, last_gram_in,
    own_sem, lcms_sem, all_send, all_recv,
    gram_send, gram_recv, right_send, right_recv, share_send, share_recv,
    fit_send, fit_recv, ng_send, ng_recv, last_send, last_recv, lg_send, lg_recv,
):
    run = lax.axis_index("run")
    mz = lax.axis_index("mz")

    def run_peer(k):
        return (lax.rem(run + k, N_RUN), mz)

    def mz_peer(k):
        return (run, lax.rem(mz + k, N_MZ))

    loads = [
        pltpu.make_async_copy(mz_hbm, mz_v, own_sem.at[0]),
        pltpu.make_async_copy(scan_hbm, scan_v, own_sem.at[1]),
        pltpu.make_async_copy(ppm_hbm, ppm_v, own_sem.at[2]),
        pltpu.make_async_copy(spectra_hbm, spectra_v, own_sem.at[3]),
    ]
    for load in loads:
        load.start()
    per_part = RUNS // LCMS_PARTS
    lcms_loads = [
        pltpu.make_async_copy(
            lcms_hbm.at[pl.ds(c * per_part, per_part)], lcms_v.at[pl.ds(c * per_part, per_part)], lcms_sem.at[c]
        )
        for c in range(LCMS_PARTS)
    ]
    for load in lcms_loads:
        load.start()

    barrier = pltpu.get_barrier_semaphore()
    for k in range(1, N_RUN):
        pl.semaphore_signal(barrier, inc=1, device_id=run_peer(k), device_id_type=MESH)
    for k in range(1, N_MZ):
        pl.semaphore_signal(barrier, inc=1, device_id=mz_peer(k), device_id_type=MESH)
    pl.semaphore_wait(barrier, N_RUN + N_MZ - 2)

    def place(ref):
        return ref.at[run // 4, :, pl.ds(pl.multiple_of(lax.rem(run, 4) * 32, 32), 32), :]

    def piece(owner):
        return spectra_hbm.at[:, :, pl.ds(pl.multiple_of(owner * OWNED, OWNED), OWNED)]

    own_piece = pltpu.make_async_copy(piece(run), place(columns_v), own_sem.at[4])
    own_piece.start()
    spread = {}
    for k in FIRST_BATCH + SECOND_BATCH + THIRD_BATCH:
        peer = run_peer(k)
        spread[k] = pltpu.make_async_remote_copy(
            src_ref=piece(peer[0]), dst_ref=place(columns_v),
            send_sem=all_send.at[k], recv_sem=all_recv.at[k], device_id=peer, device_id_type=MESH,
        )
    for k in FIRST_BATCH:
        spread[k].start()

    def exchange(peer_of, count, source_of, target, send, recv):
        copies = []
        for k in range(1, count):
            peer = peer_of(k)
            copies.append(pltpu.make_async_remote_copy(
                src_ref=source_of(peer), dst_ref=target,
                send_sem=send.at[k], recv_sem=recv.at[k], device_id=peer, device_id_type=MESH,
            ))
        for copy in copies:
            copy.start()
        return copies

    def arrive(copies):
        for copy in copies:
            copy.wait_recv()

    def total(ref, count):
        value = ref[0]
        for k in range(1, count):
            value = value + ref[k]
        return value

    for load in loads:
        load.wait()
    mz_high, mz_low = split(mz_v[...])
    mz_parts = jnp.concatenate([mz_high, mz_low], axis=0)
    mz_gram = fold(dot(mz_parts, mz_parts, NT))
    step = 1024
    sums = jnp.zeros((256, 128), F32)
    for c in range(POSITIONS // step):
        spec = jnp.concatenate([spectra_v[0, :, c * step : (c + 1) * step], spectra_v[1, :, c * step : (c + 1) * step]], axis=0)
        spec_high, spec_low = split(spec)
        ppm_high, ppm_low = split(ppm_v[:, c * step : (c + 1) * step])
        sums = sums + dot(
            jnp.concatenate([spec_high, spec_low, ppm_high, ppm_low], axis=0),
            jnp.concatenate([ppm_high, ppm_low], axis=0), NT,
        )
    nmr_local = fold(sums[0:128])
    ppm_gram = fold(sums[128:256])
    gram_in[mz] = jnp.concatenate([mz_gram, ppm_gram], axis=1)
    gram_copies = exchange(mz_peer, N_MZ, lambda peer: gram_in.at[mz], gram_in.at[mz], gram_send, gram_recv)

    scan = scan_v[...]
    scan_bf = scan.astype(BF16).astype(F32)
    scan_rows = jnp.concatenate([scan_bf, scan_bf], axis=0).T
    for c in range(LCMS_PARTS):
        lcms_loads[c].wait()
        found = []
        for i in range(per_part):
            inner = dot(lcms_v[c * per_part + i], mz_parts, NT)
            found.append(jnp.sum(inner * scan_rows, axis=0, keepdims=True))
        lcms_acc[pl.ds(c * per_part, per_part), :] = jnp.concatenate(found, axis=0)
    lcms_local = lcms_acc[:, 0:64] + lcms_acc[:, 64:128]
    lcms_packed = pack(lcms_local)
    right_in[mz] = pack(lcms_local + nmr_local)
    right_copies = exchange(mz_peer, N_MZ, lambda peer: right_in.at[mz], right_in.at[mz], right_send, right_recv)
    for k in SECOND_BATCH:
        spread[k].start()

    arrive(gram_copies)
    grams = total(gram_in, N_MZ)
    lcms_gram = dot(scan, scan, NT, HIGHEST) * grams[:, 0:64]
    first_inverse = twice(spd_inverse(lcms_gram + grams[:, 64:128]))

    arrive(right_copies)
    right_all[run] = total(right_in, N_MZ)
    share_copies = exchange(run_peer, N_RUN, lambda peer: right_all.at[run], right_all.at[run], share_send, share_recv)
    for k in THIRD_BATCH:
        spread[k].start()
    arrive(share_copies)
    first = dot(right_all[...].reshape(512, 128), first_inverse, NN, HIGHEST)
    products = dot(first, first, TN, HIGHEST)
    sample_gram = products[0:64, 0:64] + products[64:128, 64:128]
    weights = dot(first, twice(spd_inverse(sample_gram)), NN, HIGHEST).T

    own_piece.wait()
    arrive([spread[k] for k in spread])
    ppm_new = jnp.zeros((RANK, OWNED), F32)
    for g in range(4):
        rows = slice(128 * g, 128 * g + 128)
        part_high, part_low = split(jnp.concatenate([weights[0:64, rows], weights[64:128, rows]], axis=1))
        high, low = split(columns_v[g].reshape(256, OWNED))
        both = dot(jnp.concatenate([part_high, part_low], axis=0), high, NN)
        ppm_new = ppm_new + ((both[0:64] + both[64:128]) + dot(part_high, low, NN))
    new_ref[...] = ppm_new
    new_high, new_low = split(ppm_new)
    new_parts = jnp.concatenate([new_high, new_low], axis=0)
    new_gram_in[run] = pack(fold(dot(new_parts, new_parts, NT)))
    ng_copies = exchange(run_peer, N_RUN, lambda peer: new_gram_in.at[run], new_gram_in.at[run], ng_send, ng_recv)
    for g in range(4):
        high, low = split(columns_v[g].reshape(256, OWNED))
        both = dot(high, new_parts, NT) + dot(low, new_parts, NT)
        fit = both[:, 0:64] + both[:, 64:128]
        fit_out[pl.ds(4 * g, 4)] = jnp.concatenate([fit[0:128], fit[128:256]], axis=1).reshape(4, 32, 128)
    fit_in[run] = fit_out[run]
    fit_copies = exchange(run_peer, N_RUN, lambda peer: fit_out.at[peer[0]], fit_in.at[run], fit_send, fit_recv)

    arrive(ng_copies)
    last_gram_in[mz] = total(new_gram_in, N_RUN)
    lg_copies = exchange(mz_peer, N_MZ, lambda peer: last_gram_in.at[mz], last_gram_in.at[mz], lg_send, lg_recv)
    arrive(fit_copies)
    last_in[mz] = total(fit_in, N_RUN) + lcms_packed
    last_copies = exchange(mz_peer, N_MZ, lambda peer: last_in.at[mz], last_in.at[mz], last_send, last_recv)
    arrive(lg_copies)
    last_inverse = twice(spd_inverse(lcms_gram + unpack(total(last_gram_in, N_MZ))))
    arrive(last_copies)
    sample_ref[...] = unpack(dot(total(last_in, N_MZ), last_inverse, NN, HIGHEST))

    for copies in (gram_copies, right_copies, share_copies, ng_copies, fit_copies, lg_copies, last_copies):
        for copy in copies:
            copy.wait_send()
    for k in spread:
        spread[k].wait_send()


def per_device(lcms, spectra, scan_factor, mz_factor, ppm_factor):
    hbm = pl.BlockSpec(memory_space=pl.ANY)
    vmem = pl.BlockSpec(memory_space=pltpu.VMEM)
    sems = pltpu.SemaphoreType.DMA
    return pl.pallas_call(
        kernel,
        out_shape=(
            jax.ShapeDtypeStruct((RUNS, RANK), F32),
            jax.ShapeDtypeStruct((RANK, OWNED), F32),
        ),
        in_specs=[hbm] * 5,
        out_specs=(vmem, vmem),
        scratch_shapes=[
            pltpu.VMEM((RUNS, SCANS, CHANNELS), BF16),
            pltpu.VMEM((2, 32, POSITIONS), F32),
            pltpu.VMEM((RANK, SCANS), F32),
            pltpu.VMEM((RANK, CHANNELS), F32),
            pltpu.VMEM((RANK, POSITIONS), F32),
            pltpu.VMEM((RUNS, 128), F32),
            pltpu.VMEM((4, 2, 128, OWNED), F32),
            pltpu.VMEM((N_MZ, 64, 128), F32),
            pltpu.VMEM((N_MZ, 32, 128), F32),
            pltpu.VMEM((N_RUN, 32, 128), F32),
            pltpu.VMEM((N_RUN, 32, 128), F32),
            pltpu.VMEM((N_RUN, 32, 128), F32),
            pltpu.VMEM((N_RUN, 32, 128), F32),
            pltpu.VMEM((N_MZ, 32, 128), F32),
            pltpu.VMEM((N_MZ, 32, 128), F32),
            sems((5,)), sems((LCMS_PARTS,)), sems((N_RUN,)), sems((N_RUN,)),
            sems((N_MZ,)), sems((N_MZ,)), sems((N_MZ,)), sems((N_MZ,)), sems((N_RUN,)), sems((N_RUN,)),
            sems((N_RUN,)), sems((N_RUN,)), sems((N_RUN,)), sems((N_RUN,)),
            sems((N_MZ,)), sems((N_MZ,)), sems((N_MZ,)), sems((N_MZ,)),
        ],
        compiler_params=pltpu.CompilerParams(
            collective_id=0, has_side_effects=True, vmem_limit_bytes=50 * 2**20
        ),
    )(lcms, spectra.reshape(2, 32, POSITIONS), scan_factor, mz_factor, ppm_factor)


def solution(mesh):
    return jax.shard_map(
        per_device,
        mesh=mesh,
        in_specs=(P("run", None, "mz"), P("run", "mz"), P(), P(None, "mz"), P(None, "mz")),
        out_specs=(P("run", None), P(None, ("mz", "run"))),
        check_vma=False,
    )
```

time: 304 us -> 66.7 us (0.22)
  waiting for transfers between devices: 121 us -> 0 us
  blocking collectives: 99 us -> 0 us
  Pallas kernels: 0 us -> 60.3 us
  other arithmetic: 36.3 us -> 0 us
  matrix products: 32.3 us -> 0 us
  between operations: 13.9 us -> 0.65 us
  local copies, waits for them, and re-layouts: 0.96 us -> 4.6 us
    psum x2 -> x0, blocking collectives: 99 us -> none  [the longest x1 65.3 us: per_device(): lax.psum(jnp.dot(sample_first.T, sample_first, precision=highest), 'run')]
    psum x1 -> x0, waiting for transfers between devices: 76 us -> none  [per_device(): mz_gram, ppm_gram = lax.psum((mz_local, ppm_local), 'mz')]
    pallas_call x0 -> x1, Pallas kernels: none -> 60.3 us  [per_device(): pl.pallas_call(kernel, out_shape=(jax.ShapeDtypeStruct((RUNS, RANK), F32)...]
    all_gather x1 -> x0, waiting for transfers between devices: 44.6 us -> none  [per_device(): ppm_piece = lax.all_gather(ppm_new, 'run', axis=1, tiled=True)]
    another operation x15 -> x0, other arithmetic: 36.2 us -> none  [the longest x6 13 us: solve_rows(): lower_factor = jnp.linalg.cholesky(gram_matrix)]
    dot_general x9 -> x0, matrix products: 28.6 us -> none  [the longest x1 9.6 us: per_device(): jnp.einsum('ijk,rj->irk', lcms, scan_bf, preferred_element_type=jnp.float32)]
    unnamed x13 -> x8, local copies, waits for them, and re-layouts: 0.74 us -> 4.6 us
    another operation x6 -> x0, matrix products: 3.71 us -> none  [the longest x2 2.14 us: per_device(): jax.scipy.linalg.cho_solve((jnp.linalg.cholesky(sample_gram), True), proj...]
  transfers between devices with their start and end apart: 3 -> 0, of which waited for: 2 -> 0; matrix products, arithmetic and copies ran while one was open for 4% -> 0% of each run, Pallas kernels for 0% -> 0%
where the time goes in v1:
time: 66.7 us; the launch traced here: 65.5 us
  Pallas kernels  60.3 us (90%)
  local copies, waits for them, and re-layouts  4.6 us (7%)
    pallas_call x1, Pallas kernels, per_device(): pl.pallas_call(kernel, out_shape=(jax.ShapeDtypeStruct((RUNS, RANK), F32)...  60.3 us
    unnamed x8, local copies, waits for them, and re-layouts  4.6 us

profile of v1, /device:TPU:0, one launch (start us, length us, event | category | flops | bytes accessed | tf_op | source)
XLA Modules:
  0.0 65.5 jit_solution(7373976032943876420)
XLA Ops:
  0.6 0.0 copy-start
  0.6 1.6 %copy-done = f32[64,8192]{1,0:T(8,128)S(1)} copy-done((f32[64,8192]{1,0:T(8,128)S(1)}, f32[64,8192]{1,0:T(8,128)}, u32[]{:S(2)}) %copy-start) | copy-done | bytes 2097176
  2.2 0.0 copy-start.1
  2.2 0.9 %copy-done.1 = f32[64,512]{1,0:T(8,128)S(1)} copy-done((f32[64,512]{1,0:T(8,128)S(1)}, f32[64,512]{1,0:T(8,128)}, u32[]{:S(2)}) %copy-start.1) | copy-done | bytes 131096
  3.1 0.0 copy-start.2
  3.1 0.8 %copy-done.2 = f32[64,256]{1,0:T(8,128)S(1)} copy-done((f32[64,256]{1,0:T(8,128)S(1)}, f32[64,256]{1,0:T(8,128)}, u32[]{:S(2)}) %copy-start.2) | copy-done | bytes 65560
  4.0 60.3 %shard_map.68 = (f32[64,64]{1,0:T(8,128)S(1)}, f32[64,512]{1,0:T(8,128)S(1)}) custom-call(bf16[64,256,512]{2,1,0:T(8,128)(2,1)} %lcms_hbm.1, f32[2,32,8192]{2,1,0:T(8,128)S(1)} %bitcast.1, f32[64,256]{1,0:T(8,128)S(1)} %copy-done.2, f32[64,512]{1,0:T(8,128)S(1)} %copy-done.1, f32[64,8192]{1,0:T(8,128)} %ppm_hbm.1), custom_call_target="tpu_custom_call" | custom-call | tf_op jit(solution)/shard_map/pallas_call | solution.py:300
  64.3 0.6 copy.9
  64.9 0.7 copy.10
Async XLA Ops:
  0.6 1.6 %copy-start = (f32[64,8192]{1,0:T(8,128)S(1)}, f32[64,8192]{1,0:T(8,128)}, u32[]{:S(2)}) copy-start(f32[64,8192]{1,0:T(8,128)} %param.6) | copy-start | bytes 6291460
  2.2 0.9 %copy-start.1 = (f32[64,512]{1,0:T(8,128)S(1)}, f32[64,512]{1,0:T(8,128)}, u32[]{:S(2)}) copy-start(f32[64,512]{1,0:T(8,128)} %mz_hbm.1) | copy-start | bytes 393220
  3.1 0.8 %copy-start.2 = (f32[64,256]{1,0:T(8,128)S(1)}, f32[64,256]{1,0:T(8,128)}, u32[]{:S(2)}) copy-start(f32[64,256]{1,0:T(8,128)} %scan_hbm.1) | copy-start | bytes 196612

commit v2 on v1

v2 whole, which is shorter than its diff:
```python
import functools

import jax
import jax.numpy as jnp
from jax import lax
from jax.experimental import pallas as pl
from jax.experimental.pallas import tpu as pltpu
from jax.sharding import PartitionSpec as P

MESH = pl.DeviceIdType.MESH
HIGHEST = lax.Precision.HIGHEST
F32 = jnp.float32
BF16 = jnp.bfloat16
NT = (((1,), (1,)), ((), ()))
TN = (((0,), (0,)), ((), ()))
NN = (((1,), (0,)), ((), ()))

N_RUN = 16
N_MZ = 8
RANK = 64
RUNS = 64
SCANS = 256
CHANNELS = 512
POSITIONS = 8192
OWNED = 512
LCMS_PARTS = 8
HALF = 256
BATCHES = (5, 1, 2, 2, 2, 2, 2, 3, 3, 8)
ORDER = (2, 6, 8, 9, 3, 7, 10, 14, 4, 11, 15, 5, 12, 13, 1)
WAITS = (2, 2, 2, 1, 1)
STEPS = (0, 0, 0, 4, 4)
FIT_FIRST = 7


def split(value):
    high = value.astype(BF16)
    low = (value - high.astype(F32)).astype(BF16)
    return high, low


def dot(left, right, dims, precision=None):
    return lax.dot_general(left, right, dims, precision=precision, preferred_element_type=F32)


def tree(terms):
    while len(terms) > 1:
        terms = [terms[i] + terms[i + 1] if i + 1 < len(terms) else terms[i] for i in range(0, len(terms), 2)]
    return terms[0]


def small_inverse(block):
    if len(block) == 2:
        scale = 1.0 / (block[0][0] * block[1][1] - block[0][1] * block[0][1])
        off = -block[0][1] * scale
        return [[block[1][1] * scale, off], [off, block[0][0] * scale]]
    size = len(block) // 2
    half = range(size)
    upper = small_inverse([[block[i][j] for j in half] for i in half])
    cross = [[block[i][size + j] for j in half] for i in half]
    mixed = [[tree([upper[i][k] * cross[k][j] for k in half]) for j in half] for i in half]
    rest = [[None] * size for _ in half]
    for i in half:
        for j in range(i, size):
            rest[i][j] = block[size + i][size + j] - tree([cross[k][i] * mixed[k][j] for k in half])
            rest[j][i] = rest[i][j]
    lower = small_inverse(rest)
    side = [[tree([mixed[i][k] * lower[k][j] for k in half]) for j in half] for i in half]
    result = [[None] * (2 * size) for _ in range(2 * size)]
    for i in half:
        for j in half:
            if j >= i:
                result[i][j] = upper[i][j] + tree([side[i][k] * mixed[j][k] for k in half])
                result[j][i] = result[i][j]
            result[i][size + j] = -side[i][j]
            result[size + j][i] = -side[i][j]
            result[size + i][size + j] = lower[i][j]
    return result


def elimination(matrix, found, pivot=8):
    size, wide = RANK, 2 * RANK
    lane = lax.broadcasted_iota(jnp.int32, (8, wide), 1)
    sub = lax.broadcasted_iota(jnp.int32, (8, wide), 0)
    tiles = []
    for t in range(size // 8):
        unit = (lane == sub + (size + 8 * t)).astype(F32)
        left = jnp.concatenate([matrix[8 * t : 8 * t + 8], jnp.zeros((8, size), F32)], axis=1)
        tiles.append(left + unit)
    for j in range(0, size, pivot):
        home, first = j // 8, j % 8
        rows = [jnp.broadcast_to(tiles[home][first + k : first + k + 1], (8, wide)) for k in range(pivot)]
        block = [[None] * pivot for _ in range(pivot)]
        for k in range(pivot):
            for m in range(k, pivot):
                block[k][m] = jnp.broadcast_to(rows[k][:, j + m : j + m + 1], (8, wide))
                block[m][k] = block[k][m]
        inverse = small_inverse(block)
        fresh = [tree([inverse[k][m] * rows[m] for m in range(pivot)]) for k in range(pivot)]
        for t in range(size // 8):
            tile = tiles[t]
            tile = tile - tree(
                [jnp.broadcast_to(tile[:, j + k : j + k + 1], (8, wide)) * fresh[k] for k in range(pivot)]
            )
            if t == home:
                for k in range(pivot):
                    tile = jnp.where(sub == first + k, fresh[k], tile)
            tiles[t] = tile
        yield
    found.append(jnp.concatenate([tile[:, size:] for tile in tiles], axis=0))


def spd_inverse(matrix):
    found = []
    for _ in elimination(matrix, found):
        pass
    return found[0]


def pack(value):
    return jnp.concatenate([value[0:32], value[32:64]], axis=1)


def unpack(value):
    return jnp.concatenate([value[:, 0:64], value[:, 64:128]], axis=0)


def twice(value):
    empty = jnp.zeros_like(value)
    return jnp.concatenate(
        [jnp.concatenate([value, empty], axis=1), jnp.concatenate([empty, value], axis=1)], axis=0
    )


def fold(value):
    wide = value[0:64] + value[64:128]
    return wide[:, 0:64] + wide[:, 64:128]


def kernel(
    lcms_hbm, spectra_hbm, scan_hbm, mz_hbm, ppm_hbm,
    sample_ref, new_ref,
    lcms_v, spectra_v, scan_v, mz_v, ppm_v, lcms_acc, columns_v,
    gram_out, gram_in, gram_all, right_in, right_all, fit_out, fit_in, ng_out, ng_in, ng_mz, ng_all, last_in,
    own_sem, lcms_sem, all_send, all_recv,
    gram_send, gram_recv, right_send, right_recv, share_send, share_recv,
    fit_send, fit_recv, ng_send, ng_recv, last_send, last_recv, lg_send, lg_recv, back_send, back_recv, whole_send, whole_recv, pair_sem,
):
    run = lax.axis_index("run")
    mz = lax.axis_index("mz")

    def run_peer(k):
        across = lax.rem(run // 8 + k // 8, 2)
        along = lax.rem(lax.rem(run // 2, 4) + (k // 2) % 4, 4)
        core = lax.rem(run + k % 2, 2)
        return ((across * 4 + along) * 2 + core, mz)

    def mz_peer(k):
        return (run, lax.rem(mz + k, N_MZ))

    loads = [
        pltpu.make_async_copy(mz_hbm, mz_v, own_sem.at[0]),
        pltpu.make_async_copy(scan_hbm, scan_v, own_sem.at[1]),
        pltpu.make_async_copy(ppm_hbm, ppm_v, own_sem.at[2]),
        pltpu.make_async_copy(spectra_hbm, spectra_v, own_sem.at[3]),
    ]
    for load in loads:
        load.start()
    per_part = RUNS // LCMS_PARTS // 2
    lcms_loads = [
        pltpu.make_async_copy(
            lcms_hbm.at[:, pl.ds(c * per_part, per_part)], lcms_v.at[:, pl.ds(c * per_part, per_part)], lcms_sem.at[c]
        )
        for c in range(LCMS_PARTS)
    ]
    begun = []

    def fetch(count):
        for load in lcms_loads[len(begun) : len(begun) + count]:
            load.start()
            begun.append(load)

    barrier = pltpu.get_barrier_semaphore()
    for k in range(1, N_RUN):
        pl.semaphore_signal(barrier, inc=1, device_id=run_peer(k), device_id_type=MESH)
    for k in range(1, N_MZ):
        pl.semaphore_signal(barrier, inc=1, device_id=mz_peer(k), device_id_type=MESH)
    pl.semaphore_wait(barrier, N_RUN + N_MZ - 2)

    def place(half):
        return columns_v.at[half, run // 4, :, pl.ds(pl.multiple_of(lax.rem(run, 4) * 32, 32), 32), :]

    def piece(owner, half):
        start = pl.multiple_of(owner * OWNED + half * HALF, HALF)
        return spectra_hbm.at[:, :, pl.ds(start, HALF)]

    fetch(1)
    own_pieces = [pltpu.make_async_copy(piece(run, h), place(h), own_sem.at[4 + h]) for h in range(2)]
    for copy in own_pieces:
        copy.start()
    spread = [[], []]
    for h in range(2):
        for k in ORDER:
            peer = run_peer(k)
            spread[h].append(pltpu.make_async_remote_copy(
                src_ref=piece(peer[0], h), dst_ref=place(h),
                send_sem=all_send.at[h, k], recv_sem=all_recv.at[h, k], device_id=peer, device_id_type=MESH,
            ))
    waiting = spread[0] + spread[1]

    batches = list(BATCHES)
    released = []

    def release():
        for copy in waiting[len(released) : len(released) + batches.pop(0)]:
            copy.start()
            released.append(copy)

    release()

    def exchange(peer_of, count, source_of, target, send, recv):
        copies = []
        for k in range(1, count):
            peer = peer_of(k)
            copies.append(pltpu.make_async_remote_copy(
                src_ref=source_of(peer), dst_ref=target,
                send_sem=send.at[k], recv_sem=recv.at[k], device_id=peer, device_id_type=MESH,
            ))
        for copy in copies:
            copy.start()
        return copies

    def arrive(copies):
        for copy in copies:
            copy.wait_recv()

    def total(ref, count):
        value = ref[0]
        for k in range(1, count):
            value = value + ref[k]
        return value

    for load in loads:
        load.wait()
    fetch(2)
    mz_high, mz_low = split(mz_v[...])
    mz_parts = jnp.concatenate([mz_high, mz_low], axis=0)
    mz_gram = fold(dot(mz_parts, mz_parts, NT))
    step = 1024
    sums = jnp.zeros((256, 128), F32)
    for c in range(POSITIONS // step):
        if c % 3 == 2:
            fetch(1)
        spec = jnp.concatenate([spectra_v[0, :, c * step : (c + 1) * step], spectra_v[1, :, c * step : (c + 1) * step]], axis=0)
        spec_high, spec_low = split(spec)
        ppm_high, ppm_low = split(ppm_v[:, c * step : (c + 1) * step])
        sums = sums + dot(
            jnp.concatenate([spec_high, spec_low, ppm_high, ppm_low], axis=0),
            jnp.concatenate([ppm_high, ppm_low], axis=0), NT,
        )
    nmr_local = fold(sums[0:128])
    ppm_gram = fold(sums[128:256])
    gram_out[...] = jnp.concatenate([mz_gram, ppm_gram], axis=1).reshape(N_MZ, 8, 128)
    gram_in[mz] = gram_out[mz]
    gram_copies = exchange(mz_peer, N_MZ, lambda peer: gram_out.at[peer[1]], gram_in.at[mz], gram_send, gram_recv)
    release()

    scan = scan_v[...]
    scan_gram = dot(scan, scan, NT, HIGHEST)
    scan_bf = scan.astype(BF16).astype(F32)
    scan_rows = jnp.concatenate([scan_bf, scan_bf], axis=0).T
    inverse_found = []
    part = 0
    for c, parts in enumerate(WAITS):
        for load in lcms_loads[part : part + parts]:
            load.wait()
        fetch(2)
        release()
        if c == 1:
            arrive(gram_copies)
            gram_all[mz] = total(gram_in, N_MZ)
            whole_copies = exchange(mz_peer, N_MZ, lambda peer: gram_all.at[mz], gram_all.at[mz], whole_send, whole_recv)
        if c == 3:
            arrive(whole_copies)
            grams = gram_all[...].reshape(64, 128)
            lcms_gram = scan_gram * grams[:, 0:64]
            steps = elimination(lcms_gram + grams[:, 64:128], inverse_found)
        for i in range(part * per_part, (part + parts) * per_part):
            for half in range(2):
                inner = dot(lcms_v[half, i], mz_parts, NT)
                lcms_acc[half, i : i + 1, :] = jnp.sum(inner * scan_rows, axis=0, keepdims=True)
        for _ in range(STEPS[c]):
            next(steps)
        part += parts
    for _ in steps:
        pass
    first_inverse = twice(inverse_found[0])
    lcms_packed = jnp.concatenate([lcms_acc[h, :, 0:64] + lcms_acc[h, :, 64:128] for h in range(2)], axis=1)
    right_in[mz] = lcms_packed + pack(nmr_local)
    right_copies = exchange(mz_peer, N_MZ, lambda peer: right_in.at[mz], right_in.at[mz], right_send, right_recv)
    release()

    arrive(right_copies)
    chip, core = run // 2, lax.rem(run, 2)
    right_all[chip, core] = total(right_in, N_MZ)
    mine = right_all.at[chip, core]
    share_copies = exchange(lambda k: run_peer(2 * k), N_RUN // 2, lambda peer: mine, mine, share_send, share_recv)
    release()
    arrive(share_copies)
    pair_copy = pltpu.make_async_remote_copy(
        src_ref=right_all.at[:, core], dst_ref=right_all.at[:, core],
        send_sem=pair_sem.at[0], recv_sem=pair_sem.at[1], device_id=run_peer(1), device_id_type=MESH,
    )
    pair_copy.start()
    release()
    arrive([pair_copy])
    first = dot(right_all[...].reshape(512, 128), first_inverse, NN, HIGHEST)
    products = dot(first, first, TN, HIGHEST)
    sample_gram = products[0:64, 0:64] + products[64:128, 64:128]
    weights = dot(first, twice(spd_inverse(sample_gram)), NN, HIGHEST).T

    rows = [slice(128 * g, 128 * g + 128) for g in range(4)]
    blocks = [block for g in range(4) for block in (weights[0:64, rows[g]], weights[64:128, rows[g]])]
    part_high, part_low = split(jnp.concatenate(blocks, axis=1))
    part_both = jnp.concatenate([part_high, part_low], axis=0)
    new_gram = jnp.zeros((RANK, RANK), F32)
    fits = []
    for h in range(2):
        own_pieces[h].wait()
        arrive(spread[h])
        high, low = split(columns_v[h].reshape(1024, HALF))
        both = dot(part_both, high, NN)
        ppm_new = (both[0:64] + both[64:128]) + dot(part_high, low, NN)
        new_ref[:, h * HALF : (h + 1) * HALF] = ppm_new
        new_high, new_low = split(ppm_new)
        new_parts = jnp.concatenate([new_high, new_low], axis=0)
        new_gram = new_gram + fold(dot(new_parts, new_parts, NT))
        if h == 1:
            packed = pack(new_gram)
            for k in range(N_RUN):
                ng_out[k] = packed[2 * k : 2 * k + 2]
            ng_in[run] = ng_out[run]
            ng_copies = exchange(run_peer, N_RUN, lambda peer: ng_out.at[peer[0]], ng_in.at[run], ng_send, ng_recv)
        both = dot(high, new_parts, NT) + dot(low, new_parts, NT)
        for g in range(4):
            fit = both[256 * g : 256 * g + 256, 0:64] + both[256 * g : 256 * g + 256, 64:128]
            fit = jnp.concatenate([fit[0:128], fit[128:256]], axis=1)
            if h == 0:
                fits.append(fit)
            else:
                fit_out[pl.ds(4 * g, 4)] = (fits[g] + fit).reshape(4, 32, 128)
    fit_in[run] = fit_out[run]

    def fit_batch(ks):
        copies = []
        for k in ks:
            peer = run_peer(k)
            copies.append(pltpu.make_async_remote_copy(
                src_ref=fit_out.at[peer[0]], dst_ref=fit_in.at[run],
                send_sem=fit_send.at[k], recv_sem=fit_recv.at[k], device_id=peer, device_id_type=MESH,
            ))
        for copy in copies:
            copy.start()
        return copies

    fit_copies = fit_batch(ORDER[:FIT_FIRST])
    arrive(ng_copies)
    ng_mz[mz] = total(ng_in, N_RUN)
    lg_copies = exchange(mz_peer, N_MZ, lambda peer: ng_mz.at[mz], ng_mz.at[mz], lg_send, lg_recv)
    fit_copies = fit_copies + fit_batch(ORDER[FIT_FIRST:])
    arrive(lg_copies)
    ng_all[run] = total(ng_mz, N_MZ)
    back_copies = exchange(run_peer, N_RUN, lambda peer: ng_all.at[run], ng_all.at[run], back_send, back_recv)
    arrive(fit_copies)
    last_in[mz] = total(fit_in, N_RUN) + lcms_packed
    last_copies = exchange(mz_peer, N_MZ, lambda peer: last_in.at[mz], last_in.at[mz], last_send, last_recv)
    arrive(back_copies)
    new_total = unpack(jnp.concatenate([ng_all[k] for k in range(N_RUN)], axis=0))
    last_inverse = twice(spd_inverse(lcms_gram + new_total))
    arrive(last_copies)
    sample_ref[...] = unpack(dot(total(last_in, N_MZ), last_inverse, NN, HIGHEST))

    for copies in (gram_copies, whole_copies, right_copies, share_copies, [pair_copy], ng_copies, fit_copies, lg_copies, back_copies, last_copies, waiting):
        for copy in copies:
            copy.wait_send()


def per_device(lcms, spectra, scan_factor, mz_factor, ppm_factor):
    hbm = pl.BlockSpec(memory_space=pltpu.HBM)
    vmem = pl.BlockSpec(memory_space=pltpu.VMEM)
    sems = pltpu.SemaphoreType.DMA
    return pl.pallas_call(
        kernel,
        out_shape=(
            jax.ShapeDtypeStruct((RUNS, RANK), F32),
            jax.ShapeDtypeStruct((RANK, OWNED), F32),
        ),
        in_specs=[hbm] * 5,
        out_specs=(vmem, vmem),
        scratch_shapes=[
            pltpu.VMEM((2, 32, SCANS, CHANNELS), BF16),
            pltpu.VMEM((2, 32, POSITIONS), F32),
            pltpu.VMEM((RANK, SCANS), F32),
            pltpu.VMEM((RANK, CHANNELS), F32),
            pltpu.VMEM((RANK, POSITIONS), F32),
            pltpu.VMEM((2, 32, 128), F32),
            pltpu.VMEM((2, 4, 2, 128, HALF), F32),
            pltpu.VMEM((N_MZ, 8, 128), F32),
            pltpu.VMEM((N_MZ, 8, 128), F32),
            pltpu.VMEM((N_MZ, 8, 128), F32),
            pltpu.VMEM((N_MZ, 32, 128), F32),
            pltpu.VMEM((N_RUN // 2, 2, 32, 128), F32),
            pltpu.VMEM((N_RUN, 32, 128), F32),
            pltpu.VMEM((N_RUN, 32, 128), F32),
            pltpu.VMEM((N_RUN, 2, 128), F32),
            pltpu.VMEM((N_RUN, 2, 128), F32),
            pltpu.VMEM((N_MZ, 2, 128), F32),
            pltpu.VMEM((N_RUN, 2, 128), F32),
            pltpu.VMEM((N_MZ, 32, 128), F32),
            sems((6,)), sems((LCMS_PARTS,)), sems((2, N_RUN)), sems((2, N_RUN)),
            sems((N_MZ,)), sems((N_MZ,)), sems((N_MZ,)), sems((N_MZ,)), sems((N_RUN,)), sems((N_RUN,)),
            sems((N_RUN,)), sems((N_RUN,)), sems((N_RUN,)), sems((N_RUN,)),
            sems((N_MZ,)), sems((N_MZ,)), sems((N_MZ,)), sems((N_MZ,)), sems((N_RUN,)), sems((N_RUN,)),
            sems((N_MZ,)), sems((N_MZ,)), sems((2,)),
        ],
        compiler_params=pltpu.CompilerParams(
            collective_id=0, has_side_effects=True, vmem_limit_bytes=60 * 2**20
        ),
    )(lcms.reshape(2, 32, SCANS, CHANNELS), spectra.reshape(2, 32, POSITIONS), scan_factor, mz_factor, ppm_factor)


def solution(mesh):
    return jax.shard_map(
        per_device,
        mesh=mesh,
        in_specs=(P("run", None, "mz"), P("run", "mz"), P(), P(None, "mz"), P(None, "mz")),
        out_specs=(P("run", None), P(None, ("mz", "run"))),
        check_vma=False,
    )
```

time: 66.7 us -> 65 us (0.975)
  local copies, waits for them, and re-layouts: 4.6 us -> 2.94 us
    unnamed x8 -> x2, local copies, waits for them, and re-layouts: 4.6 us -> 2.94 us
where the time goes in v2:
time: 65 us; the launch traced here: 63.8 us
  Pallas kernels  60.2 us (93%)
  local copies, waits for them, and re-layouts  2.94 us (5%)
    pallas_call x1, Pallas kernels, per_device(): pl.pallas_call(kernel, out_shape=(jax.ShapeDtypeStruct((RUNS, RANK), F32)...  60.2 us
    unnamed x2, local copies, waits for them, and re-layouts  2.94 us

profile of v2, /device:TPU:0, one launch (start us, length us, event | category | flops | bytes accessed | tf_op | source)
XLA Modules:
  0.0 63.8 jit_solution(9894532119372397925)
XLA Ops:
  0.6 60.2 %shard_map.68 = (f32[64,64]{1,0:T(8,128)}, f32[64,512]{1,0:T(8,128)}) custom-call(bf16[2,32,256,512]{3,2,1,0:T(8,128)(2,1)} %bitcast.2, f32[2,32,8192]{2,1,0:T(8,128)} %bitcast.3, f32[64,256]{1,0:T(8,128)} %scan_hbm.1, f32[64,512]{1,0:T(8,128)} %mz_hbm.1, f32[64,8192]{1,0:T(8,128)} %ppm_hbm.1), custom_call_target="tpu_custom_call" | custom-call | tf_op jit(solution)/shard_map/pallas_call | solution.py:391
  60.8 1.4 %copy.9 = f32[64,64]{1,0:T(8,128)} copy(f32[64,64]{1,0:T(8,128)} %get-tuple-element.4) | data formatting | bytes 32768
  62.2 1.6 %copy.10 = f32[64,512]{1,0:T(8,128)} copy(f32[64,512]{1,0:T(8,128)} %get-tuple-element.5) | data formatting | bytes 262144

commit v3 on v2

--- a/solution.py
+++ b/solution.py
@@ -29,7 +29,6 @@
 ORDER = (2, 6, 8, 9, 3, 7, 10, 14, 4, 11, 15, 5, 12, 13, 1)
 WAITS = (2, 2, 2, 1, 1)
 STEPS = (0, 0, 0, 4, 4)
-FIT_FIRST = 7
 
 
 def split(value):
@@ -140,7 +139,7 @@
     lcms_hbm, spectra_hbm, scan_hbm, mz_hbm, ppm_hbm,
     sample_ref, new_ref,
     lcms_v, spectra_v, scan_v, mz_v, ppm_v, lcms_acc, columns_v,
-    gram_out, gram_in, gram_all, right_in, right_all, fit_out, fit_in, ng_out, ng_in, ng_mz, ng_all, last_in,
+    gram_out, gram_in, gram_all, right_in, right_all, fit_out, pair_in, fit_mine, fit_in, ng_out, ng_in, ng_mz, ng_all, last_in,
     own_sem, lcms_sem, all_send, all_recv,
     gram_send, gram_recv, right_send, right_recv, share_send, share_recv,
     fit_send, fit_recv, ng_send, ng_recv, last_send, last_recv, lg_send, lg_recv, back_send, back_recv, whole_send, whole_recv, pair_sem,
@@ -347,31 +346,26 @@
             if h == 0:
                 fits.append(fit)
             else:
-                fit_out[pl.ds(4 * g, 4)] = (fits[g] + fit).reshape(4, 32, 128)
-    fit_in[run] = fit_out[run]
-
-    def fit_batch(ks):
-        copies = []
-        for k in ks:
-            peer = run_peer(k)
-            copies.append(pltpu.make_async_remote_copy(
-                src_ref=fit_out.at[peer[0]], dst_ref=fit_in.at[run],
-                send_sem=fit_send.at[k], recv_sem=fit_recv.at[k], device_id=peer, device_id_type=MESH,
-            ))
-        for copy in copies:
-            copy.start()
-        return copies
-
-    fit_copies = fit_batch(ORDER[:FIT_FIRST])
+                fit_out[pl.ds(2 * g, 2)] = (fits[g] + fit).reshape(2, 2, 32, 128)
+    fit_pair = pltpu.make_async_remote_copy(
+        src_ref=fit_out.at[:, 1 - core], dst_ref=pair_in,
+        send_sem=pair_sem.at[2], recv_sem=pair_sem.at[3], device_id=run_peer(1), device_id_type=MESH,
+    )
+    fit_pair.start()
+    arrive([fit_pair])
+    fit_mine[...] = fit_out[:, core] + pair_in[...]
+    fit_in[chip] = fit_mine[chip]
+    fit_copies = exchange(
+        lambda k: run_peer(2 * k), N_RUN // 2, lambda peer: fit_mine.at[peer[0] // 2], fit_in.at[chip], fit_send, fit_recv
+    )
     arrive(ng_copies)
     ng_mz[mz] = total(ng_in, N_RUN)
     lg_copies = exchange(mz_peer, N_MZ, lambda peer: ng_mz.at[mz], ng_mz.at[mz], lg_send, lg_recv)
-    fit_copies = fit_copies + fit_batch(ORDER[FIT_FIRST:])
     arrive(lg_copies)
     ng_all[run] = total(ng_mz, N_MZ)
     back_copies = exchange(run_peer, N_RUN, lambda peer: ng_all.at[run], ng_all.at[run], back_send, back_recv)
     arrive(fit_copies)
-    last_in[mz] = total(fit_in, N_RUN) + lcms_packed
+    last_in[mz] = total(fit_in, N_RUN // 2) + lcms_packed
     last_copies = exchange(mz_peer, N_MZ, lambda peer: last_in.at[mz], last_in.at[mz], last_send, last_recv)
     arrive(back_copies)
     new_total = unpack(jnp.concatenate([ng_all[k] for k in range(N_RUN)], axis=0))
@@ -379,21 +373,27 @@
     arrive(last_copies)
     sample_ref[...] = unpack(dot(total(last_in, N_MZ), last_inverse, NN, HIGHEST))
 
-    for copies in (gram_copies, whole_copies, right_copies, share_copies, [pair_copy], ng_copies, fit_copies, lg_copies, back_copies, last_copies, waiting):
+    for copies in (gram_copies, whole_copies, right_copies, share_copies, [pair_copy, fit_pair], ng_copies, fit_copies, lg_copies, back_copies, last_copies, waiting):
         for copy in copies:
             copy.wait_send()
+
+
+def deliver(sample_ref, new_ref, sample_out, new_out):
+    sample_out[...] = sample_ref[...]
+    new_out[...] = new_ref[...]
 
 
 def per_device(lcms, spectra, scan_factor, mz_factor, ppm_factor):
     hbm = pl.BlockSpec(memory_space=pltpu.HBM)
     vmem = pl.BlockSpec(memory_space=pltpu.VMEM)
     sems = pltpu.SemaphoreType.DMA
-    return pl.pallas_call(
+    shapes = (
+        jax.ShapeDtypeStruct((RUNS, RANK), F32),
+        jax.ShapeDtypeStruct((RANK, OWNED), F32),
+    )
+    results = pl.pallas_call(
         kernel,
-        out_shape=(
-            jax.ShapeDtypeStruct((RUNS, RANK), F32),
-            jax.ShapeDtypeStruct((RANK, OWNED), F32),
-        ),
+        out_shape=shapes,
         in_specs=[hbm] * 5,
         out_specs=(vmem, vmem),
         scratch_shapes=[
@@ -409,8 +409,10 @@
             pltpu.VMEM((N_MZ, 8, 128), F32),
             pltpu.VMEM((N_MZ, 32, 128), F32),
             pltpu.VMEM((N_RUN // 2, 2, 32, 128), F32),
-            pltpu.VMEM((N_RUN, 32, 128), F32),
-            pltpu.VMEM((N_RUN, 32, 128), F32),
+            pltpu.VMEM((N_RUN // 2, 2, 32, 128), F32),
+            pltpu.VMEM((N_RUN // 2, 32, 128), F32),
+            pltpu.VMEM((N_RUN // 2, 32, 128), F32),
+            pltpu.VMEM((N_RUN // 2, 32, 128), F32),
             pltpu.VMEM((N_RUN, 2, 128), F32),
             pltpu.VMEM((N_RUN, 2, 128), F32),
             pltpu.VMEM((N_MZ, 2, 128), F32),
@@ -420,12 +422,18 @@
             sems((N_MZ,)), sems((N_MZ,)), sems((N_MZ,)), sems((N_MZ,)), sems((N_RUN,)), sems((N_RUN,)),
             sems((N_RUN,)), sems((N_RUN,)), sems((N_RUN,)), sems((N_RUN,)),
             sems((N_MZ,)), sems((N_MZ,)), sems((N_MZ,)), sems((N_MZ,)), sems((N_RUN,)), sems((N_RUN,)),
-            sems((N_MZ,)), sems((N_MZ,)), sems((2,)),
+            sems((N_MZ,)), sems((N_MZ,)), sems((4,)),
         ],
         compiler_params=pltpu.CompilerParams(
             collective_id=0, has_side_effects=True, vmem_limit_bytes=60 * 2**20
         ),
     )(lcms.reshape(2, 32, SCANS, CHANNELS), spectra.reshape(2, 32, POSITIONS), scan_factor, mz_factor, ppm_factor)
+    return pl.pallas_call(
+        deliver,
+        out_shape=shapes,
+        in_specs=[vmem] * 2,
+        out_specs=(vmem, vmem),
+    )(*results)
 
 
 def solution(mesh):

time: 65 us -> 63.5 us (0.977)
  local copies, waits for them, and re-layouts: 2.94 us -> 0 us
  Pallas kernels: 60.2 us -> 61.7 us
    unnamed x2 -> x0, local copies, waits for them, and re-layouts: 2.94 us -> none
    pallas_call x1 -> x2, Pallas kernels: 60.2 us -> 61.7 us  [the longest x1 60.1 us: per_device(): pl.pallas_call(kernel, out_shape=shapes, in_specs=[hbm] * 5, out_specs=(v...]
where the time goes in v3:
time: 63.5 us; the launch traced here: 62.4 us
  Pallas kernels  61.7 us (97%)
  between operations  0.64 us (1%)
    pallas_call x1, Pallas kernels, per_device(): pl.pallas_call(kernel, out_shape=shapes, in_specs=[hbm] * 5, out_specs=(v...  60.1 us
    pallas_call x1, Pallas kernels, per_device(): pl.pallas_call(deliver, out_shape=shapes, in_specs=[vmem] * 2, out_specs=...  1.59 us

profile of v3, /device:TPU:0, one launch (start us, length us, event | category | flops | bytes accessed | tf_op | source)
XLA Modules:
  0.0 62.4 jit_solution(14818441724200501306)
XLA Ops:
  0.6 60.1 %shard_map.68 = (f32[64,64]{1,0:T(8,128)}, f32[64,512]{1,0:T(8,128)}) custom-call(bf16[2,32,256,512]{3,2,1,0:T(8,128)(2,1)} %bitcast.2, f32[2,32,8192]{2,1,0:T(8,128)} %bitcast.3, f32[64,256]{1,0:T(8,128)} %scan_hbm.1, f32[64,512]{1,0:T(8,128)} %mz_hbm.1, f32[64,8192]{1,0:T(8,128)} %ppm_hbm.1), custom_call_target="tpu_custom_call" | custom-call | tf_op jit(solution)/shard_map/pallas_call | solution.py:394
  60.8 1.6 %shard_map.69 = (f32[64,64]{1,0:T(8,128)}, f32[64,512]{1,0:T(8,128)}) custom-call(f32[64,64]{1,0:T(8,128)} %get-tuple-element.4.sample_ref, f32[64,512]{1,0:T(8,128)} %get-tuple-element.5.new_ref), custom_call_target="tpu_custom_call" | custom-call | tf_op jit(solution)/shard_map/pallas_call | solution.py:431

commit v4 on v3

--- a/solution.py
+++ b/solution.py
@@ -352,15 +352,15 @@
         send_sem=pair_sem.at[2], recv_sem=pair_sem.at[3], device_id=run_peer(1), device_id_type=MESH,
     )
     fit_pair.start()
+    arrive(ng_copies)
+    ng_mz[mz] = total(ng_in, N_RUN)
+    lg_copies = exchange(mz_peer, N_MZ, lambda peer: ng_mz.at[mz], ng_mz.at[mz], lg_send, lg_recv)
     arrive([fit_pair])
     fit_mine[...] = fit_out[:, core] + pair_in[...]
     fit_in[chip] = fit_mine[chip]
     fit_copies = exchange(
         lambda k: run_peer(2 * k), N_RUN // 2, lambda peer: fit_mine.at[peer[0] // 2], fit_in.at[chip], fit_send, fit_recv
     )
-    arrive(ng_copies)
-    ng_mz[mz] = total(ng_in, N_RUN)
-    lg_copies = exchange(mz_peer, N_MZ, lambda peer: ng_mz.at[mz], ng_mz.at[mz], lg_send, lg_recv)
     arrive(lg_copies)
     ng_all[run] = total(ng_mz, N_MZ)
     back_copies = exchange(run_peer, N_RUN, lambda peer: ng_all.at[run], ng_all.at[run], back_send, back_recv)

time: 63.5 us -> 63.5 us (level)
  no operation moved by 1% of the time
where the time goes in v4:
time: 63.5 us; the launch traced here: 62.4 us
  Pallas kernels  61.7 us (97%)
  between operations  0.64 us (1%)
    pallas_call x1, Pallas kernels, per_device(): pl.pallas_call(kernel, out_shape=shapes, in_specs=[hbm] * 5, out_specs=(v...  60.1 us
    pallas_call x1, Pallas kernels, per_device(): pl.pallas_call(deliver, out_shape=shapes, in_specs=[vmem] * 2, out_specs=...  1.59 us

profile of v4, /device:TPU:0, one launch (start us, length us, event | category | flops | bytes accessed | tf_op | source)
XLA Modules:
  0.0 62.4 jit_solution(796276697206640125)
XLA Ops:
  0.6 60.1 %shard_map.68 = (f32[64,64]{1,0:T(8,128)}, f32[64,512]{1,0:T(8,128)}) custom-call(bf16[2,32,256,512]{3,2,1,0:T(8,128)(2,1)} %bitcast.2, f32[2,32,8192]{2,1,0:T(8,128)} %bitcast.3, f32[64,256]{1,0:T(8,128)} %scan_hbm.1, f32[64,512]{1,0:T(8,128)} %mz_hbm.1, f32[64,8192]{1,0:T(8,128)} %ppm_hbm.1), custom_call_target="tpu_custom_call" | custom-call | tf_op jit(solution)/shard_map/pallas_call | solution.py:394
  60.8 1.6 %shard_map.69 = (f32[64,64]{1,0:T(8,128)}, f32[64,512]{1,0:T(8,128)}) custom-call(f32[64,64]{1,0:T(8,128)} %get-tuple-element.4.sample_ref, f32[64,512]{1,0:T(8,128)} %get-tuple-element.5.new_ref), custom_call_target="tpu_custom_call" | custom-call | tf_op jit(solution)/shard_map/pallas_call | solution.py:431
